TPU v7x, 256 devices: a whole 4x4x8 slice. The times are simulated.
256 devices in a mesh: dp: 8 (over z), expert: 32 (over x, y, core).
Axes of the slice: x: 4, y: 4, z: 8, core: 2. Of those that a mesh axis runs over, the one named last changes fastest.
Arguments:
- tokens: bfloat16 [32768, 2048], P(('dp', 'expert')), parts along dimension 0, may hold values from -6 to 6
- routes: int32 [32768, 8], P(('dp', 'expert')), parts along dimension 0, may hold values from 0 to 31, all different within a row; in each aligned block of 128 rows (0 to 127, 128 to 255, ...) at most 40 rows name the same one
- gate_num: int32 [32768, 8], P(('dp', 'expert')), parts along dimension 0, may hold values from 1 to 1023
- w_gate: bfloat16 [32, 2048, 768], P('expert'), may hold values from -0.125 to 0.125
- w_up: bfloat16 [32, 2048, 768], P('expert'), may hold values from -0.125 to 0.125
- w_down: bfloat16 [32, 768, 2048], P('expert'), may hold values from -0.21875 to 0.21875
Outputs:
- combined: bfloat16 [32768, 2048], P(('dp', 'expert')), parts along dimension 0
There are 8 independent parts, one for each index of `dp`. A program takes and returns all parts, laid end to end along the dimension named above; an argument that names none is the same for every part. Nothing has to cross between parts.
Inputs may be any that keep to these rules, and one draw needn't show every extreme that they name: `routes`: each row names 8 different experts; among the rows of one device no expert is named more than 40 times, a bound that some block reaches.
All inputs are finite; a program needn't handle non-finite values.
Results may differ from a plain program's by a relative error of at most 0.0057.
Values may be sent and summed in bfloat16 or wider, within the bound.
No kernel may reach another device: no remote copies, remote signals or barrier semaphores. Data moves between devices by JAX's collectives and lax.ppermute only.
A program may use at most 128 MiB of HBM per device.

v0:
```python
import jax
import jax.numpy as jnp
from jax import lax
from jax.sharding import PartitionSpec as P

GATE_DEN = 1024


def expert_apply(rows, w_gate, w_up, w_down):
    gate_part = jnp.einsum("srd,dh->srh", rows, w_gate[0], preferred_element_type=jnp.float32)
    up_part = jnp.einsum("srd,dh->srh", rows, w_up[0], preferred_element_type=jnp.float32)
    hidden = (jax.nn.silu(gate_part) * up_part).astype(jnp.bfloat16)
    return jnp.einsum("srh,hd->srd", hidden, w_down[0], preferred_element_type=jnp.float32).astype(
        jnp.bfloat16
    )


def send_back(outputs):
    return lax.all_to_all(outputs, "expert", split_axis=0, concat_axis=0, tiled=True)


def body(tokens, routes, gate_num, w_gate, w_up, w_down):
    group_size = lax.axis_size("expert")
    tok_dev = tokens.shape[0]
    top_count = routes.shape[1]
    capacity = min(tok_dev, 5 * tok_dev * top_count // (4 * group_size))
    expert_range = jnp.arange(group_size, dtype=jnp.int32)
    slot_range = jnp.arange(capacity, dtype=jnp.int32)
    onehot = jnp.any(routes[:, :, None] == expert_range[None, None, :], axis=1).astype(jnp.int32)
    slots = jnp.cumsum(onehot, axis=0) - 1
    all_rows = lax.all_gather(tokens, "expert", axis=0, tiled=True)
    all_routes = lax.all_gather(routes, "expert", axis=0, tiled=True)
    own_expert = lax.axis_index("expert")
    routed = (
        jnp.any(all_routes == own_expert, axis=1).astype(jnp.int32).reshape(group_size, tok_dev)
    )
    all_slots = jnp.cumsum(routed, axis=1) - 1
    selector = (
        (routed[:, None, :] == 1) & (all_slots[:, None, :] == slot_range[None, :, None])
    ).astype(jnp.bfloat16)
    grouped = all_rows.reshape(group_size, tok_dev, all_rows.shape[1])
    buffer = jnp.einsum(
        "sct,std->scd", selector, grouped, preferred_element_type=jnp.float32
    ).astype(jnp.bfloat16)
    returned = send_back(expert_apply(buffer, w_gate, w_up, w_down))
    returned_flat = returned.reshape(group_size * capacity, returned.shape[2])
    slot_chosen = jnp.take_along_axis(slots, routes, axis=1)
    flat_slot = routes * capacity + slot_chosen
    picked = returned_flat[flat_slot]
    weights = gate_num.astype(jnp.float32) / GATE_DEN
    combined = jnp.sum(picked.astype(jnp.float32) * weights[:, :, None], axis=1)
    return combined.astype(jnp.bfloat16)


def solution(mesh):
    placed = (
        P(("dp", "expert"), None),
        P(("dp", "expert"), None),
        P(("dp", "expert"), None),
        P("expert", None, None),
        P("expert", None, None),
        P("expert", None, None),
    )
    return jax.shard_map(
        body, mesh=mesh, in_specs=placed, out_specs=P(("dp", "expert"), None), check_vma=False
    )
```

profile of v0, /device:TPU:8, one launch (start us, length us, event | category | flops | bytes accessed | tf_op | source)
XLA Modules:
  0.0 225.0 jit_solution(1968779918979069390)
XLA Ops:
  6.5 0.0 copy-start
  6.5 0.0 all-gather.2.cloned.1.call-start
  6.5 0.7 all-gather.2.cloned.1.call-update
  7.3 24.6 %all_gather.6 = s32[4096,8]{0,1:T(8,128)S(1)} all-gather(s32[128,8]{0,1:T(8,128)} %param.7), channel_id=1, replica_groups=mesh['dp'=8,'expert'=32] {'expert'}, dimensions={0}, use_global_device_ids=true | all-gather | bytes 135168 | tf_op jit(solution)/shard_map/all_gather | solution.py:32
  31.9 0.1 compare_reduce_fusion
  31.9 0.3 reduce_window_sum.22
  32.3 57.7 %all-gather.2.cloned.1.call-done = bf16[4096,2048]{1,0:T(8,128)(2,1)} async-done(((bf16[128,2048]{1,0:T(8,128)(2,1)}), bf16[4096,2048]{1,0:T(8,128)(2,1)}) %all-gather.2.cloned.1.call-update) | async-done | bytes 16777232 | tf_op jit(solution)/shard_map/all_gather | solution.py:31
  90.0 0.0 copy-start.4
  90.0 8.2 %convolution_convert_fusion.1 = bf16[32,40,2048]{2,1,0:T(8,128)(2,1)S(1)} fusion(bf16[32,128,2048]{2,1,0:T(8,128)(2,1)} %bitcast.32, s32[32,128]{1,0:T(8,128)S(1)} %broadcast_add_fusion.1, pred[32,128]{1,0:T(8,128)(4,1)S(1)} %broadcast_compare_fusion), kind=kOutput, calls=%fused_computation.5 | convolution fusion | flops 674037760 | bytes 22040576 | tf_op jit(solution)/shard_map/sct,std->scd/dot_general | solution.py:42
  98.2 0.0 copy-start.1
  98.2 2.3 %copy-done.1 = bf16[32,40,2048]{2,1,0:T(8,128)(2,1)} copy-done((bf16[32,40,2048]{2,1,0:T(8,128)(2,1)}, bf16[32,40,2048]{2,1,0:T(8,128)(2,1)S(1)}, u32[]{:S(2)}) %copy-start.1) | copy-done | bytes 5242904
  100.6 0.0 copy-done.4
  100.6 6.4 %fusion.2 = f32[32,40,768]{2,1,0:T(8,128)} fusion(bf16[32,40,2048]{2,1,0:T(8,128)(2,1)S(1)} %convolution_convert_fusion.1, bf16[1,2048,768]{2,1,0:T(8,128)(2,1)S(1)} %copy-done.4), kind=kOutput, calls=%fused_computation.8 | convolution fusion | flops 4026531840 | bytes 12320768 | tf_op jit(solution)/shard_map/srd,dh->srh/dot_general | solution.py:11
  107.0 0.0 copy-done
  107.0 14.7 %convolution_convert_fusion = bf16[32,40,2048]{2,1,0:T(8,128)(2,1)} fusion(bf16[1,768,2048]{2,1,0:T(8,128)(2,1)S(1)} %copy-done, f32[32,40,768]{2,1,0:T(8,128)} %fusion.2, bf16[32,40,2048]{2,1,0:T(8,128)(2,1)} %copy-done.1, bf16[1,2048,768]{2,1,0:T(8,128)(2,1)} %param.9), kind=kOutput, calls=%fused_computation.4 | convolution fusion | flops 8061583360 | bytes 20709376 | tf_op jit(solution)/shard_map/srh,hd->srd/dot_general | solution.py:13
  121.7 0.0 copy-start.2
  121.7 6.2 %all-to-all-start = ((bf16[32,40,2048]{2,1,0:T(8,128)(2,1)}), bf16[32,40,2048]{2,1,0:T(8,128)(2,1)}, u32[]{:S(2)}, u32[]{:S(2)}) async-start(bf16[32,40,2048]{2,1,0:T(8,128)(2,1)} %convolution_convert_fusion), calls=%async_computation | async-start | bytes 10485760 | tf_op jit(solution)/shard_map/all_to_all | solution.py:19
  128.0 0.0 copy-done.2
  128.0 0.1 copy.27
  128.1 0.2 reduce_window_sum.23
  128.3 0.1 copy.28
  128.4 0.1 reshape.53
  128.5 0.0 copy-start.3
  128.5 7.1 %gather_fusion.1 = s32[1024]{0:T(1024)S(1)} fusion(s32[128,32]{1,0:T(8,128)S(1)} %broadcast_add_fusion, s32[1024]{0:T(1024)S(1)} %reshape.53), kind=kCustom, calls=%fused_computation.1 | custom fusion | bytes 16384 | tf_op jit(solution)/shard_map/jit(take_along_axis)/gather | solution.py:47
  135.6 0.1 reshape.56
  135.7 0.1 copy.30
  135.9 0.1 reshape.47
  136.0 0.0 copy-done.3
  136.0 0.1 copy.31
  136.1 62.8 %all-to-all-done = bf16[32,40,2048]{2,1,0:T(8,128)(2,1)} async-done(((bf16[32,40,2048]{2,1,0:T(8,128)(2,1)}), bf16[32,40,2048]{2,1,0:T(8,128)(2,1)}, u32[]{:S(2)}, u32[]{:S(2)}) %all-to-all-start) | async-done | bytes 5242912 | tf_op jit(solution)/shard_map/all_to_all | solution.py:19
  198.9 12.0 %gather_fusion = bf16[1024,2048]{1,0:T(8,128)(2,1)} fusion(bf16[1280,2048]{1,0:T(8,128)(2,1)} %bitcast.8, s32[1024]{0:T(1024)S(1)} %broadcast_clamp_fusion), kind=kCustom, calls=%fused_computation | custom fusion | bytes 8392704 | tf_op jit(solution)/shard_map/gather | solution.py:49
  210.9 7.3 %fusion = bf16[128,2048]{1,0:T(8,128)(2,1)} fusion(bf16[1024,2048]{1,0:T(8,128)(2,1)} %gather_fusion, f32[128,8]{1,0:T(8,128)S(1)} %copy.31), kind=kLoop, calls=%fused_computation.3 | loop fusion | flops 6029312 | bytes 4722688 | tf_op jit(solution)/shard_map/reduce_sum | solution.py:51
  (11 shorter events, 0.1 us)
Async XLA Ops:
  6.5 100.5 %copy-start = (bf16[1,768,2048]{2,1,0:T(8,128)(2,1)S(1)}, bf16[1,768,2048]{2,1,0:T(8,128)(2,1)}, u32[]{:S(2)}) copy-start(bf16[1,768,2048]{2,1,0:T(8,128)(2,1)} %param.11) | copy-start | bytes 9437188
  6.5 83.5 %all-gather.2.cloned.1.call-start = ((), (), s32[]{:S(2)}) async-start(), calls=%async_computation.1 | async-start | bytes 17301504 | tf_op jit(solution)/shard_map/all_gather | solution.py:31
  90.0 10.6 %copy-start.4 = (bf16[1,2048,768]{2,1,0:T(8,128)(2,1)S(1)}, bf16[1,2048,768]{2,1,0:T(8,128)(2,1)}, u32[]{:S(2)}) copy-start(bf16[1,2048,768]{2,1,0:T(8,128)(2,1)} %param.10) | copy-start | bytes 9437188
  98.2 2.3 %copy-start.1 = (bf16[32,40,2048]{2,1,0:T(8,128)(2,1)}, bf16[32,40,2048]{2,1,0:T(8,128)(2,1)S(1)}, u32[]{:S(2)}) copy-start(bf16[32,40,2048]{2,1,0:T(8,128)(2,1)S(1)} %convolution_convert_fusion.1) | copy-start | bytes 15728644
  121.7 6.3 %copy-start.2 = (s32[128,8]{0,1:T(8,128)S(1)}, s32[128,8]{0,1:T(8,128)}, u32[]{:S(2)}) copy-start(s32[128,8]{0,1:T(8,128)} %param.7) | copy-start | bytes 12292
  121.7 77.2 %all-to-all-start = ((bf16[32,40,2048]{2,1,0:T(8,128)(2,1)}), bf16[32,40,2048]{2,1,0:T(8,128)(2,1)}, u32[]{:S(2)}, u32[]{:S(2)}) async-start(bf16[32,40,2048]{2,1,0:T(8,128)(2,1)} %convolution_convert_fusion), calls=%async_computation | async-start | bytes 10485760 | tf_op jit(solution)/shard_map/all_to_all | solution.py:19
  128.5 7.5 %copy-start.3 = (s32[128,8]{0,1:T(8,128)S(1)}, s32[128,8]{0,1:T(8,128)}, u32[]{:S(2)}) copy-start(s32[128,8]{0,1:T(8,128)} %param.8) | copy-start | bytes 12292
Sparse Core Ops, SparseCore 0:
  9.9 80.0 all-gather.1
where the time goes:
time: 225 us
  waiting for transfers between devices  121 us (54%)
  matrix products  29.3 us (13%)
  blocking collectives  24.6 us (11%)
  local copies, waits for them, and re-layouts  22.1 us (10%)
  between operations  13.5 us (6%)
  other arithmetic  7.91 us (4%)
  starting transfers between devices  6.25 us (3%)
    all_to_all x1, waiting for transfers between devices, send_back(): lax.all_to_all(outputs, 'expert', split_axis=0, concat_axis=0, tiled=True)  62.8 us
    all_gather x1, waiting for transfers between devices, body(): all_rows = lax.all_gather(tokens, 'expert', axis=0, tiled=True)  57.7 us
    all_gather x1, blocking collectives, body(): all_routes = lax.all_gather(routes, 'expert', axis=0, tiled=True)  24.6 us
    dot_general x1, matrix products, expert_apply(): jnp.einsum('srh,hd->srd', hidden, w_down[0], preferred_element_type=jnp.f...  14.7 us
    gather x1, local copies, waits for them, and re-layouts, body(): picked = returned_flat[flat_slot]  12 us
    dot_general x1, matrix products, body(): jnp.einsum('sct,std->scd', selector, grouped, preferred_element_type=jnp....  8.22 us
    gather x5, local copies, waits for them, and re-layouts, body(): slot_chosen = jnp.take_along_axis(slots, routes, axis=1)  7.39 us
    reduce_sum x1, other arithmetic, body(): combined = jnp.sum(picked.astype(jnp.float32) * weights[:, :, None], axis=1)  7.33 us
  transfers between devices with their start and end apart: 2, of which 2 were waited for; matrix products, arithmetic and copies ran while one was open for 4% of the time, Pallas kernels for 0%

commit v1 on v0

--- a/solution.py
+++ b/solution.py
@@ -28,8 +28,11 @@
     slot_range = jnp.arange(capacity, dtype=jnp.int32)
     onehot = jnp.any(routes[:, :, None] == expert_range[None, None, :], axis=1).astype(jnp.int32)
     slots = jnp.cumsum(onehot, axis=0) - 1
-    all_rows = lax.all_gather(tokens, "expert", axis=0, tiled=True)
-    all_routes = lax.all_gather(routes, "expert", axis=0, tiled=True)
+    all_rows, all_routes = jnp.split(
+        lax.all_gather(jnp.concatenate([tokens, routes], axis=1), "expert", axis=0, tiled=True),
+        [tokens.shape[1]],
+        axis=1,
+    )
     own_expert = lax.axis_index("expert")
     routed = (
         jnp.any(all_routes == own_expert, axis=1).astype(jnp.int32).reshape(group_size, tok_dev)

time: 225 us -> 252 us (1.12)
  waiting for transfers between devices: 121 us -> 153 us
  blocking collectives: 24.6 us -> 0 us
  local copies, waits for them, and re-layouts: 22.1 us -> 36.4 us
  other arithmetic: 7.91 us -> 13.2 us
    all_gather x1, waiting for transfers between devices: 57.7 us -> 82.5 us  [body(): lax.all_gather(jnp.concatenate([tokens, routes], axis=1), 'expert', axis=...]
    all_gather x1 -> x0, blocking collectives: 24.6 us -> none  [body(): all_routes = lax.all_gather(routes, 'expert', axis=0, tiled=True)]
    split x0 -> x1, local copies, waits for them, and re-layouts: none -> 14.1 us  [body(): jnp.split(lax.all_gather(jnp.concatenate([tokens, routes], axis=1), 'expe...]
    all_to_all x1, waiting for transfers between devices: 62.8 us -> 70.6 us  [send_back(): lax.all_to_all(outputs, 'expert', split_axis=0, concat_axis=0, tiled=True)]
  transfers between devices with their start and end apart: 2 -> 2, of which waited for: 2 -> 2; matrix products, arithmetic and copies ran while one was open for 4% -> 0% of each run, Pallas kernels for 0% -> 0%
where the time goes in v1:
time: 252 us
  waiting for transfers between devices  153 us (61%)
  local copies, waits for them, and re-layouts  36.4 us (14%)
  matrix products  29.3 us (12%)
  between operations  13.5 us (5%)
  other arithmetic  13.2 us (5%)
  starting transfers between devices  6.46 us (3%)
    all_gather x1, waiting for transfers between devices, body(): lax.all_gather(jnp.concatenate([tokens, routes], axis=1), 'expert', axis=...  82.5 us
    all_to_all x1, waiting for transfers between devices, send_back(): lax.all_to_all(outputs, 'expert', split_axis=0, concat_axis=0, tiled=True)  70.6 us
    dot_general x1, matrix products, expert_apply(): jnp.einsum('srh,hd->srd', hidden, w_down[0], preferred_element_type=jnp.f...  14.7 us
    split x1, local copies, waits for them, and re-layouts, body(): jnp.split(lax.all_gather(jnp.concatenate([tokens, routes], axis=1), 'expe...  14.1 us
    gather x1, local copies, waits for them, and re-layouts, body(): picked = returned_flat[flat_slot]  12 us
    dot_general x1, matrix products, body(): jnp.einsum('sct,std->scd', selector, grouped, preferred_element_type=jnp....  8.22 us
    gather x5, local copies, waits for them, and re-layouts, body(): slot_chosen = jnp.take_along_axis(slots, routes, axis=1)  7.39 us
    reduce_sum x1, other arithmetic, body(): combined = jnp.sum(picked.astype(jnp.float32) * weights[:, :, None], axis=1)  7.33 us
  transfers between devices with their start and end apart: 2, of which 2 were waited for; matrix products, arithmetic and copies ran while one was open for 0% of the time, Pallas kernels for 0%

profile of v1, /device:TPU:8, one launch (start us, length us, event | category | flops | bytes accessed | tf_op | source)
XLA Modules:
  0.0 252.0 jit_solution(631670656871008008)
XLA Ops:
  6.5 0.0 copy-start
  6.5 0.0 all-gather.2.cloned.1.call-start
  6.5 0.9 fusion.14
  7.4 0.8 bitcast_or_fusion
  8.2 0.1 copy.31
  8.3 0.2 reduce_window_sum.23
  8.5 0.1 copy.32
  8.6 0.1 reshape.53
  8.7 0.0 copy-start.2
  8.7 7.1 %gather_fusion.1 = s32[1024]{0:T(1024)S(1)} fusion(s32[128,32]{1,0:T(8,128)S(1)} %broadcast_add_fusion, s32[1024]{0:T(1024)S(1)} %reshape.53), kind=kCustom, calls=%fused_computation.1 | custom fusion | bytes 16384 | tf_op jit(solution)/shard_map/jit(take_along_axis)/gather | solution.py:50
  15.8 0.1 reshape.56
  15.9 0.0 copy-done.2
  15.9 0.1 copy.30
  16.1 1.9 pad_maximum_fusion
  18.0 0.0 all-gather.2.cloned.1.call-update
  18.0 82.5 %all-gather.2.cloned.1.call-done = bf16[4096,2056]{1,0:T(8,128)(2,1)} async-done(((bf16[128,2056]{1,0:T(8,128)(2,1)}), bf16[4096,2056]{1,0:T(8,128)(2,1)}) %all-gather.2.cloned.1.call-update) | async-done | bytes 16842768 | tf_op jit(solution)/shard_map/all_gather | solution.py:32
  100.5 1.8 compare_reduce_fusion
  102.4 0.3 reduce_window_sum.22
  102.7 14.1 %split.9 = bf16[4096,2048]{1,0:T(8,128)(2,1)} slice(bf16[4096,2056]{1,0:T(8,128)(2,1)} %all-gather.2.cloned.1.call-done), slice={[0:4096], [0:2048]} | slice | bytes 33554432 | tf_op jit(solution)/shard_map/split | solution.py:31
  116.8 8.2 %convolution_convert_fusion.1 = bf16[32,40,2048]{2,1,0:T(8,128)(2,1)S(1)} fusion(bf16[32,128,2048]{2,1,0:T(8,128)(2,1)} %bitcast.32, s32[32,128]{1,0:T(8,128)S(1)} %broadcast_add_fusion.1, pred[32,128]{1,0:T(8,128)(4,1)S(1)} %broadcast_compare_fusion), kind=kOutput, calls=%fused_computation.5 | convolution fusion | flops 674037760 | bytes 22040576 | tf_op jit(solution)/shard_map/sct,std->scd/dot_general | solution.py:45
  125.0 0.0 copy-start.1
  125.0 2.3 copy-done.1
  127.4 0.0 copy-done.4
  127.4 6.4 %fusion.2 = f32[32,40,768]{2,1,0:T(8,128)} fusion(bf16[32,40,2048]{2,1,0:T(8,128)(2,1)S(1)} %convolution_convert_fusion.1, bf16[1,2048,768]{2,1,0:T(8,128)(2,1)S(1)} %copy-done.4), kind=kOutput, calls=%fused_computation.8 | convolution fusion | flops 4026531840 | bytes 12320768 | tf_op jit(solution)/shard_map/srd,dh->srh/dot_general | solution.py:11
  133.8 14.7 %convolution_convert_fusion = bf16[32,40,2048]{2,1,0:T(8,128)(2,1)} fusion(bf16[1,768,2048]{2,1,0:T(8,128)(2,1)S(1)} %copy-done, f32[32,40,768]{2,1,0:T(8,128)} %fusion.2, bf16[32,40,2048]{2,1,0:T(8,128)(2,1)} %copy-done.1, bf16[1,2048,768]{2,1,0:T(8,128)(2,1)} %param.9), kind=kOutput, calls=%fused_computation.4 | convolution fusion | flops 8061583360 | bytes 20709376 | tf_op jit(solution)/shard_map/srh,hd->srd/dot_general | solution.py:13
  148.5 6.5 %all-to-all-start = ((bf16[32,40,2048]{2,1,0:T(8,128)(2,1)}), bf16[32,40,2048]{2,1,0:T(8,128)(2,1)}, u32[]{:S(2)}, u32[]{:S(2)}) async-start(bf16[32,40,2048]{2,1,0:T(8,128)(2,1)} %convolution_convert_fusion), calls=%async_computation | async-start | bytes 10485760 | tf_op jit(solution)/shard_map/all_to_all | solution.py:19
  155.0 0.1 copy.34
  155.1 0.1 reshape.47
  155.2 0.1 copy.35
  155.3 70.6 %all-to-all-done = bf16[32,40,2048]{2,1,0:T(8,128)(2,1)} async-done(((bf16[32,40,2048]{2,1,0:T(8,128)(2,1)}), bf16[32,40,2048]{2,1,0:T(8,128)(2,1)}, u32[]{:S(2)}, u32[]{:S(2)}) %all-to-all-start) | async-done | bytes 5242912 | tf_op jit(solution)/shard_map/all_to_all | solution.py:19
  225.9 12.0 %gather_fusion = bf16[1024,2048]{1,0:T(8,128)(2,1)} fusion(bf16[1280,2048]{1,0:T(8,128)(2,1)} %bitcast.8, s32[1024]{0:T(1024)S(1)} %broadcast_clamp_fusion), kind=kCustom, calls=%fused_computation | custom fusion | bytes 8392704 | tf_op jit(solution)/shard_map/gather | solution.py:52
  237.8 7.3 %fusion = bf16[128,2048]{1,0:T(8,128)(2,1)} fusion(bf16[1024,2048]{1,0:T(8,128)(2,1)} %gather_fusion, f32[128,8]{1,0:T(8,128)S(1)} %copy.35), kind=kLoop, calls=%fused_computation.3 | loop fusion | flops 6029312 | bytes 4722688 | tf_op jit(solution)/shard_map/reduce_sum | solution.py:54
  (13 shorter events, 0.1 us)
Async XLA Ops:
  6.5 127.3 %copy-start = (bf16[1,768,2048]{2,1,0:T(8,128)(2,1)S(1)}, bf16[1,768,2048]{2,1,0:T(8,128)(2,1)}, u32[]{:S(2)}) copy-start(bf16[1,768,2048]{2,1,0:T(8,128)(2,1)} %param.11) | copy-start | bytes 9437188
  6.5 94.0 %all-gather.2.cloned.1.call-start = ((), (), s32[]{:S(2)}) async-start(), calls=%async_computation.1 | async-start | bytes 18382848 | tf_op jit(solution)/shard_map/all_gather | solution.py:32
  8.7 7.2 %copy-start.2 = (s32[128,8]{0,1:T(8,128)S(1)}, s32[128,8]{0,1:T(8,128)}, u32[]{:S(2)}) copy-start(s32[128,8]{0,1:T(8,128)} %param.7) | copy-start | bytes 12292
  116.8 10.6 %copy-start.4 = (bf16[1,2048,768]{2,1,0:T(8,128)(2,1)S(1)}, bf16[1,2048,768]{2,1,0:T(8,128)(2,1)}, u32[]{:S(2)}) copy-start(bf16[1,2048,768]{2,1,0:T(8,128)(2,1)} %param.10) | copy-start | bytes 9437188
  125.0 2.3 copy-start.1
  148.5 6.7 %copy-start.3 = (s32[128,8]{0,1:T(8,128)S(1)}, s32[128,8]{0,1:T(8,128)}, u32[]{:S(2)}) copy-start(s32[128,8]{0,1:T(8,128)} %param.8) | copy-start | bytes 12292
  148.5 77.4 %all-to-all-start = ((bf16[32,40,2048]{2,1,0:T(8,128)(2,1)}), bf16[32,40,2048]{2,1,0:T(8,128)(2,1)}, u32[]{:S(2)}, u32[]{:S(2)}) async-start(bf16[32,40,2048]{2,1,0:T(8,128)(2,1)} %convolution_convert_fusion), calls=%async_computation | async-start | bytes 10485760 | tf_op jit(solution)/shard_map/all_to_all | solution.py:19
Sparse Core Ops, SparseCore 0:
  18.1 82.3 all-gather.1
